TPU v7x, 512 devices: a whole 4x8x8 slice. The times are simulated.
512 devices in a mesh: blk: 64 (over y, z_hi, core), head: 8 (over z_lo, x).
Axes of the slice: x: 4, y: 8, z: 8 (z_hi: 4, z_lo: 2; z = z_hi * 2 + z_lo), core: 2. Of those that a mesh axis runs over, the one named last changes fastest.
Arguments:
- query_nope: bfloat16 [4096, 8192], P('blk', 'head'), may hold values from -140 to 140
- query_rope: bfloat16 [4096, 4096], P('blk', 'head'), may hold values from -6 to 6
- compressed: bfloat16 [4096, 576], P(('blk', 'head')), may hold values from -6 to 6
- latent_gain: float32 [512], replicated, may hold values from 0.1 to 1.9
- key_up: bfloat16 [64, 128, 512], P('head'), may hold values from -0.5 to 0.5
- value_up: bfloat16 [64, 512, 128], P('head'), may hold values from -1.5 to 1.5
- span_order: int32 [128], replicated, may hold values from 0 to 127, each once
Outputs:
- attended: bfloat16 [4096, 8192], P('blk', 'head')
Inputs may be any that keep to these rules, and one draw needn't show every extreme that they name: Every number appears once; device index i of blk holds the blocks span_order[2 i] and span_order[2 i + 1].
All inputs are finite; a program needn't handle non-finite values.
Results may differ from a plain program's by a relative error of at most 0.0075.
The roundings to bfloat16 on the way count: a program that leaves them out, or rounds other values in their place, can miss the bound.
Values may be sent and summed in bfloat16 or wider, within the bound.
No kernel may reach another device: no remote copies, remote signals or barrier semaphores. Data moves between devices by JAX's collectives and lax.ppermute only.
A program may use at most 64 MiB of HBM per device.

v0:
```python
import jax
import jax.numpy as jnp
from jax import lax
from jax.sharding import Mesh
from jax.sharding import PartitionSpec as P

BLK = ("blk_0", "blk_1", "blk_2")
BLK_HEAD = ("blk_0", "blk_1", "blk_2", "head")
norm_epsilon = 1e-06
rope_base = 10000.0
masked_score = -1e30


def joined_along(parts, dim):
    parts = jnp.moveaxis(parts, 0, dim)
    dims = parts.shape
    return parts.reshape(*dims[:dim], dims[dim] * dims[dim + 1], *dims[dim + 2 :])


def from_everyone(value, axis):
    size = lax.axis_size(axis)
    return lax.all_to_all(
        jnp.broadcast_to(value[None], (size, *value.shape)), axis, 0, 0, tiled=True
    )


def collect(value, axis, dim):
    return joined_along(from_everyone(value, axis), dim)


def stacked_from(value, axes, order):
    parts = value[None]
    for k in order:
        parts = lax.all_gather(parts, axes[k], axis=0, tiled=True)
    block = [lax.axis_size(axes[k]) for k in reversed(order)]
    parts = parts.reshape(*block, *value.shape)
    turned = sorted(range(len(order)), key=lambda place: order[len(order) - 1 - place])
    return parts.transpose(*turned, *range(len(order), parts.ndim)).reshape(-1, *value.shape)


def whole_of(value, axes, order, dim):
    return joined_along(stacked_from(value, axes, order), dim)


def lookup(entries, index_array):
    slots = jnp.arange(entries.shape[0], dtype=jnp.int32)
    matches = index_array[..., None] == slots
    return jnp.sum(jnp.where(matches, entries, 0), axis=-1)


def rotate(values, positions):
    half_width = values.shape[-1] // 2
    frequency = rope_base ** (-jnp.arange(half_width, dtype=jnp.float32) / half_width)
    angles = positions.astype(jnp.float32)[..., None] * frequency
    cosine = jnp.cos(angles)
    sine_value = jnp.sin(angles)
    leading = values[..., :half_width]
    trailing = values[..., half_width:]
    return jnp.concatenate(
        [leading * cosine - trailing * sine_value, leading * sine_value + trailing * cosine],
        axis=-1,
    )


def shards(query_nope, query_rope, compressed, latent_gain, key_up, value_up, span_order):
    tokens_here = query_nope.shape[0]
    heads_here = key_up.shape[0]
    nope_width = key_up.shape[1]
    latent_width = key_up.shape[2]
    rope_width = query_rope.shape[1] // heads_here
    value_width = value_up.shape[2]
    half_block = tokens_here // 2
    slice_count = compressed.shape[0]
    block_id = lax.axis_index(BLK)
    head_id = lax.axis_index("head")

    def positions_of(row_ids):
        return lookup(span_order, row_ids // half_block) * half_block + row_ids % half_block

    query_pos = positions_of(block_id * tokens_here + jnp.arange(tokens_here, dtype=jnp.int32))
    own_rows = (
        block_id * tokens_here + head_id * slice_count + jnp.arange(slice_count, dtype=jnp.int32)
    )
    own_pos = positions_of(own_rows)
    latent = compressed[:, :latent_width].astype(jnp.float32)
    latent = (
        latent
        * lax.rsqrt(jnp.mean(latent * latent, axis=1, keepdims=True) + norm_epsilon)
        * latent_gain
    )
    latent = latent.astype(jnp.bfloat16)
    key_rot = rotate(compressed[:, latent_width:].astype(jnp.float32), own_pos).astype(jnp.bfloat16)
    key_rows = jnp.concatenate([latent, key_rot], axis=1)
    nope_parts = query_nope.reshape(tokens_here, heads_here, nope_width)
    query_lat = jnp.einsum(
        "thn,hnl->thl", nope_parts, key_up, preferred_element_type=jnp.float32
    ).astype(jnp.bfloat16)
    query_rot = rotate(
        query_rope.reshape(tokens_here, heads_here, rope_width).astype(jnp.float32),
        query_pos[:, None],
    ).astype(jnp.bfloat16)
    row_count = tokens_here * heads_here
    queries = jnp.concatenate([query_lat, query_rot], axis=2).reshape(
        row_count, latent_width + rope_width
    )
    query_rows_pos = jnp.repeat(query_pos, heads_here)
    score_scale = (nope_width + rope_width) ** (-0.5)
    block_keys = collect(key_rows, "head", 0)
    shard_keys = whole_of(block_keys, BLK, (1, 0, 2), 0)
    row_ids = jnp.arange(shard_keys.shape[0], dtype=jnp.int32)
    run_max = jnp.full((row_count,), masked_score, jnp.float32)
    scores = (
        jnp.einsum("qd,kd->qk", queries, shard_keys, preferred_element_type=jnp.float32)
        * score_scale
    )
    visible = positions_of(row_ids)[None, :] <= query_rows_pos[:, None]
    scores = jnp.where(visible, scores, masked_score)
    new_max = jnp.maximum(run_max, jnp.max(scores, axis=1))
    weight = jnp.where(visible, jnp.exp(scores - new_max[:, None]), 0.0)
    new_sum = jnp.sum(weight, axis=1)
    product = jnp.dot(
        weight.astype(jnp.bfloat16),
        shard_keys[:, :latent_width],
        preferred_element_type=jnp.float32,
    )
    folded = (new_max, new_sum, product)
    run_max, run_sum, run_acc = folded
    lat_out = (
        (run_acc / run_sum[:, None])
        .astype(jnp.bfloat16)
        .reshape(tokens_here, heads_here, latent_width)
    )
    attended = jnp.einsum(
        "thl,hlv->thv", lat_out, value_up, preferred_element_type=jnp.float32
    ).astype(jnp.bfloat16)
    return attended.reshape(tokens_here, heads_here * value_width)


def solution(mesh):
    split = Mesh(
        mesh.devices.reshape(8, 4, 2, mesh.shape["head"]), ("blk_0", "blk_1", "blk_2", "head")
    )
    placed = (
        P(BLK, "head"),
        P(BLK, "head"),
        P(BLK_HEAD, None),
        P(),
        P("head", None, None),
        P("head", None, None),
        P(),
    )
    return jax.shard_map(
        shards, mesh=split, in_specs=placed, out_specs=P(BLK, "head"), check_vma=False
    )
```

profile of v0, /device:TPU:1, one launch (start us, length us, event | category | flops | bytes accessed | tf_op | source)
XLA Modules:
  0.0 131.8 jit_solution(17058499181964433245)
XLA Ops:
  6.5 0.0 copy-start
  6.5 0.0 copy-start.2
  6.5 0.0 all-gather.3.cloned.1.call-start
  6.6 0.9 fusion.34
  7.5 0.7 slice_convert_fusion
  8.2 0.8 select_reduce_fusion.2
  9.0 0.8 fusion.36
  9.8 0.1 fusion.44
  9.9 0.1 pad_maximum_fusion.1
  10.0 11.7 %all_to_all.5 = bf16[8,8,576]{2,1,0:T(8,128)(2,1)S(1)} all-to-all(bf16[8,8,576]{2,1,0:T(8,128)(2,1)S(1)} %broadcast_in_dim.66), channel_id=1, replica_groups=mesh['blk_0'=8,'blk_1'=4,'blk_2'=2,'head'=8] {'head'}, dimensions={0} | all-to-all | bytes 147456 | tf_op jit(solution)/shard_map/all_to_all | solution.py:22
  21.7 18.8 %all_gather.9 = bf16[4,64,576]{2,1,0:T(8,128)(2,1)} all-gather(bf16[1,64,576]{2,1,0:T(8,128)(2,1)S(1)} %bitcast.33), channel_id=1, replica_groups=mesh['blk_0'=8,'blk_1'=4,'blk_2'=2,'head'=8] {'blk_1'}, dimensions={0}, use_global_device_ids=true | all-gather | bytes 368640 | tf_op jit(solution)/shard_map/all_gather | solution.py:34
  40.5 0.0 all-gather.3.cloned.1.call-update
  40.5 0.0 all-gather.5.cloned.1.call-start
  40.6 42.2 %all-gather.3.cloned.1.call-done = bf16[32,64,576]{2,1,0:T(8,128)(2,1)} async-done(((bf16[4,64,576]{2,1,0:T(8,128)(2,1)}), bf16[32,64,576]{2,1,0:T(8,128)(2,1)}) %all-gather.3.cloned.1.call-update) | async-done | bytes 2359312 | tf_op jit(solution)/shard_map/all_gather | solution.py:34
  82.8 0.0 all-gather.5.cloned.1.call-update
  82.8 0.8 select_reduce_fusion.1
  83.7 0.1 broadcast_in_dim.63
  83.8 0.1 le.16
  83.9 1.0 reshape.213
  84.9 0.2 multiply_cosine_fusion
  85.1 0.1 fusion.55
  85.2 0.1 subtract_convert_fusion
  85.3 0.0 copy-done
  85.3 1.2 fusion.11
  86.5 0.1 pad_maximum_fusion
  86.6 0.0 copy-done.2
  86.7 1.3 select_reduce_fusion
  88.0 23.6 %all-gather.5.cloned.1.call-done = bf16[64,64,576]{2,1,0:T(8,128)(2,1)} async-done(((bf16[32,64,576]{2,1,0:T(8,128)(2,1)}), bf16[64,64,576]{2,1,0:T(8,128)(2,1)}) %all-gather.5.cloned.1.call-update) | async-done | bytes 4718608 | tf_op jit(solution)/shard_map/all_gather | solution.py:34
  111.6 3.0 %copy.34 = bf16[8,4,2,64,576]{4,3,2,1,0:T(8,128)(2,1)S(1)} copy(bf16[8,4,2,64,576]{4,3,1,0,2:T(8,128)(2,1)} %bitcast.30) | data formatting | bytes 9437184 | tf_op jit(solution)/shard_map/transpose | solution.py:38
  114.7 4.0 %fusion = (f32[512]{0:T(512)S(1)}, f32[512,4096]{1,0:T(8,128)S(1)}) fusion(s32[4096]{0:T(1024)S(1)} %fusion.37, s32[512]{0:T(512)S(1)} %le.16, bf16[4096,576]{1,0:T(8,128)(2,1)S(1)} %bitcast.31, bf16[64,8,576]{2,0,1:T(8,128)(2,1)S(1)} %pad_maximum_fusion), kind=kOutput, calls=%fused_computation.2 | convolution fusion | flops 2424307200 | bytes 13717504 | tf_op jit(solution)/shard_map/qd,kd->qk/dot_general | solution.py:113
  118.7 2.6 %fusion.1 = f32[512]{0:T(512)S(1)} fusion(f32[512,4096]{1,0:T(8,128)S(1)} %get-tuple-element.16, f32[512]{0:T(512)S(1)} %broadcast_maximum_fusion, s32[4096]{0:T(1024)S(1)} %fusion.37, s32[512]{0:T(512)S(1)} %le.16), kind=kLoop, calls=%fused_computation.3 | loop fusion | flops 12582400 | bytes 8411136 | tf_op jit(solution)/shard_map/reduce_sum | solution.py:120
  121.3 0.0 copy-start.1
  121.3 2.6 %fusion.17 = bf16[64,8,512]{2,1,0:T(8,128)(2,1)S(1)} fusion(bf16[4096,576]{1,0:T(8,128)(2,1)S(1)} %bitcast.32, f32[512,4096]{1,0:T(8,128)S(1)} %get-tuple-element.16, f32[512]{0:T(512)S(1)} %broadcast_maximum_fusion, s32[4096]{0:T(1024)S(1)} %fusion.37, s32[512]{0:T(512)S(1)} %le.16, f32[512]{0:T(512)S(1)} %fusion.1), kind=kOutput, calls=%fused_computation.19 | convolution fusion | flops 2160590848 | bytes 13129728 | tf_op jit(solution)/shard_map/dot_general | solution.py:121
  123.9 0.0 copy-done.1
  123.9 0.4 fusion.12
  124.3 0.7 copy.58
  (10 shorter events, 0.1 us)
Async XLA Ops:
  6.5 78.8 %copy-start = (bf16[8,128,512]{2,1,0:T(8,128)(2,1)S(1)}, bf16[8,128,512]{2,1,0:T(8,128)(2,1)}, u32[]{:S(2)}) copy-start(bf16[8,128,512]{2,1,0:T(8,128)(2,1)} %param.11) | copy-start | bytes 3145732
  6.5 80.1 %copy-start.2 = (s32[128]{0:T(128)S(1)}, s32[128]{0:T(128)}, u32[]{:S(2)}) copy-start(s32[128]{0:T(128)} %param.13) | copy-start | bytes 1540
  6.5 76.3 %all-gather.3.cloned.1.call-start = ((), (), s32[]{:S(2)}) async-start(), calls=%async_computation.1 | async-start | bytes 2949120 | tf_op jit(solution)/shard_map/all_gather | solution.py:34
  40.5 71.1 %all-gather.5.cloned.1.call-start = ((), (), s32[]{:S(2)}) async-start(), calls=%async_computation.2 | async-start | bytes 7864320 | tf_op jit(solution)/shard_map/all_gather | solution.py:34
  121.3 2.6 %copy-start.1 = (bf16[8,512,128]{2,1,0:T(8,128)(2,1)S(1)}, bf16[8,512,128]{2,1,0:T(8,128)(2,1)}, u32[]{:S(2)}) copy-start(bf16[8,512,128]{2,1,0:T(8,128)(2,1)} %param.12) | copy-start | bytes 3145732
Sparse Core Ops, SparseCore 0:
  40.6 42.1 all-gather.2
  84.9 26.6 all-gather.4
where the time goes:
time: 132 us
  waiting for transfers between devices  65.9 us (50%)
  blocking collectives  30.5 us (23%)
  between operations  13.5 us (10%)
  other arithmetic  8.63 us (7%)
  matrix products  8.16 us (6%)
  local copies, waits for them, and re-layouts  5.02 us (4%)
    all_gather x2, waiting for transfers between devices, stacked_from(): parts = lax.all_gather(parts, axes[k], axis=0, tiled=True)  65.9 us
    all_gather x1, blocking collectives, stacked_from(): parts = lax.all_gather(parts, axes[k], axis=0, tiled=True)  18.8 us
    all_to_all x1, blocking collectives, from_everyone(): lax.all_to_all(jnp.broadcast_to(value[None], (size, *value.shape)), axis,...  11.7 us
    dot_general x1, matrix products, shards(): jnp.einsum('qd,kd->qk', queries, shard_keys, preferred_element_type=jnp.f...  4.03 us
    transpose x1, local copies, waits for them, and re-layouts, stacked_from(): parts.transpose(*turned, *range(len(order), parts.ndim))  3.05 us
    reduce_sum x3, other arithmetic, lookup(): return jnp.sum(jnp.where(matches, entries, 0), axis=-1)  2.95 us
  transfers between devices with their start and end apart: 2, of which 2 were waited for; matrix products, arithmetic and copies ran while one was open for 4% of the time, Pallas kernels for 0%

commit v1 on v0

--- a/solution.py
+++ b/solution.py
@@ -31,7 +31,16 @@
 def stacked_from(value, axes, order):
     parts = value[None]
     for k in order:
-        parts = lax.all_gather(parts, axes[k], axis=0, tiled=True)
+        obj = axes[k]
+        parts = jnp.concatenate(
+            jax.lax.all_to_all(
+                jnp.stack([parts for _ in range(jax.lax.axis_size(obj))], axis=0),
+                axis_name=obj,
+                split_axis=0,
+                concat_axis=0,
+            ),
+            0,
+        )
     block = [lax.axis_size(axes[k]) for k in reversed(order)]
     parts = parts.reshape(*block, *value.shape)
     turned = sorted(range(len(order)), key=lambda place: order[len(order) - 1 - place])

time: 132 us -> 127 us (0.962)
  between operations: 13.5 us -> 0.17 us
  blocking collectives: 30.5 us -> 41.6 us
  waiting for transfers between devices: 65.9 us -> 56.1 us
  starting transfers between devices: 0.04 us -> 6.82 us
  other arithmetic: 8.63 us -> 11.3 us
    all_gather x2 -> x0, waiting for transfers between devices: 65.9 us -> none  [stacked_from(): parts = lax.all_gather(parts, axes[k], axis=0, tiled=True)]
    all_to_all x0 -> x1, waiting for transfers between devices: none -> 56.1 us  [stacked_from(): jax.lax.all_to_all(jnp.stack([parts for _ in range(jax.lax.axis_size(obj)...]
    all_to_all x0 -> x2, blocking collectives: none -> 29.9 us  [stacked_from(): jax.lax.all_to_all(jnp.stack([parts for _ in range(jax.lax.axis_size(obj)...]
    all_gather x1 -> x0, blocking collectives: 18.8 us -> none  [stacked_from(): parts = lax.all_gather(parts, axes[k], axis=0, tiled=True)]
    all_to_all x0 -> x1, starting transfers between devices: none -> 6.82 us  [stacked_from(): jax.lax.all_to_all(jnp.stack([parts for _ in range(jax.lax.axis_size(obj)...]
    another operation x2 -> x3, other arithmetic: 0.22 us -> 3.52 us  [the longest x1 3.31 us: stacked_from(): jnp.stack([parts for _ in range(jax.lax.axis_size(obj))], axis=0)]
    transpose x1 -> x0, local copies, waits for them, and re-layouts: 3.05 us -> none  [stacked_from(): parts.transpose(*turned, *range(len(order), parts.ndim))]
    another operation x0 -> x3, local copies, waits for them, and re-layouts: none -> 2.57 us  [the longest x2 1.92 us: stacked_from(): jnp.stack([parts for _ in range(jax.lax.axis_size(obj))], axis=0)]
  transfers between devices with their start and end apart: 2 -> 1, of which waited for: 2 -> 1; matrix products, arithmetic and copies ran while one was open for 4% -> 2% of each run, Pallas kernels for 0% -> 0%
where the time goes in v1:
time: 127 us
  waiting for transfers between devices  56.1 us (44%)
  blocking collectives  41.6 us (33%)
  other arithmetic  11.3 us (9%)
  matrix products  7.2 us (6%)
  starting transfers between devices  6.82 us (5%)
  local copies, waits for them, and re-layouts  3.7 us (3%)
    all_to_all x1, waiting for transfers between devices, stacked_from(): jax.lax.all_to_all(jnp.stack([parts for _ in range(jax.lax.axis_size(obj)...  56.1 us
    all_to_all x2, blocking collectives, stacked_from(): jax.lax.all_to_all(jnp.stack([parts for _ in range(jax.lax.axis_size(obj)...  29.9 us
    all_to_all x1, blocking collectives, from_everyone(): lax.all_to_all(jnp.broadcast_to(value[None], (size, *value.shape)), axis,...  11.7 us
    all_to_all x1, starting transfers between devices, stacked_from(): jax.lax.all_to_all(jnp.stack([parts for _ in range(jax.lax.axis_size(obj)...  6.82 us
    dot_general x1, matrix products, shards(): jnp.einsum('qd,kd->qk', queries, shard_keys, preferred_element_type=jnp.f...  3.93 us
    another operation x1, other arithmetic, stacked_from(): jnp.stack([parts for _ in range(jax.lax.axis_size(obj))], axis=0)  3.31 us
    reduce_sum x1, other arithmetic, shards(): new_sum = jnp.sum(weight, axis=1)  2.62 us
    dot_general x1, matrix products, shards(): jnp.dot(weight.astype(jnp.bfloat16), shard_keys[:, :latent_width], prefer...  2.6 us
  transfers between devices with their start and end apart: 1, of which 1 were waited for; matrix products, arithmetic and copies ran while one was open for 2% of the time, Pallas kernels for 0%

profile of v1, /device:TPU:1, one launch (start us, length us, event | category | flops | bytes accessed | tf_op | source)
XLA Modules:
  0.0 126.8 jit_solution(16265638979630070881)
XLA Ops:
  0.0 0.0 copy-start
  0.0 0.0 copy-start.4
  0.0 0.0 copy-start.3
  0.0 0.0 copy-start.2
  0.0 0.9 fusion.34
  0.9 0.7 slice_convert_fusion
  1.6 0.8 select_reduce_fusion.2
  2.5 0.8 fusion.36
  3.3 0.1 fusion.44
  3.4 0.1 pad_maximum_fusion.2
  3.5 11.7 %all_to_all.20 = bf16[8,8,576]{2,1,0:T(8,128)(2,1)S(1)} all-to-all(bf16[8,8,576]{2,1,0:T(8,128)(2,1)S(1)} %broadcast_in_dim.66), channel_id=1, replica_groups=mesh['blk_0'=8,'blk_1'=4,'blk_2'=2,'head'=8] {'head'}, dimensions={0} | all-to-all | bytes 147456 | tf_op jit(solution)/shard_map/all_to_all | solution.py:22
  15.2 17.6 %all_to_all.21 = bf16[4,1,64,576]{3,2,1,0:T(8,128)(2,1)S(1)} all-to-all(bf16[4,1,64,576]{3,2,1,0:T(8,128)(2,1)S(1)} %stack.9), channel_id=1, replica_groups=mesh['blk_0'=8,'blk_1'=4,'blk_2'=2,'head'=8] {'blk_1'}, dimensions={0} | all-to-all | bytes 589824 | tf_op jit(solution)/shard_map/all_to_all | solution.py:36
  32.8 1.9 %stack.10 = bf16[8,4,64,576]{3,2,1,0:T(8,128)(2,1)} broadcast(bf16[4,64,576]{2,1,0:T(8,128)(2,1)S(1)} %bitcast.35), dimensions={1,2,3} | broadcast | bytes 2654208 | tf_op jit(solution)/shard_map/stack | solution.py:37
  34.7 6.8 %all-to-all-start.2 = ((bf16[8,4,64,576]{3,2,1,0:T(8,128)(2,1)}), bf16[8,4,64,576]{3,2,1,0:T(8,128)(2,1)}, u32[]{:S(2)}, u32[]{:S(2)}) async-start(bf16[8,4,64,576]{3,2,1,0:T(8,128)(2,1)} %stack.10), calls=%async_computation.2 | async-start | bytes 5242880 | tf_op jit(solution)/shard_map/all_to_all | solution.py:36
  41.6 0.0 copy-done.4
  41.6 0.2 select_reduce_fusion.1
  41.8 0.1 broadcast_in_dim.63
  41.8 0.1 le.16
  41.9 0.0 copy-done.3
  42.0 0.1 reshape.215
  42.1 0.2 multiply_cosine_fusion
  42.3 0.1 fusion.55
  42.4 0.1 subtract_convert_fusion
  42.5 0.0 copy-done
  42.5 0.0 copy-done.2
  42.6 0.3 fusion.11
  42.9 0.1 pad_maximum_fusion.1
  43.0 1.3 %select_reduce_fusion = s32[4096]{0:T(1024)S(1)} fusion(s32[128]{0:T(128)S(1)} %copy-done.4, s32[4096]{0:T(1024)S(1)} %add_select_fusion), kind=kLoop, calls=%fused_computation.13 | loop fusion | flops 1568768 | bytes 33280 | tf_op jit(solution)/shard_map/reduce_sum | solution.py:57
  44.3 56.1 %all-to-all-done.2 = bf16[8,4,64,576]{3,2,1,0:T(8,128)(2,1)} async-done(((bf16[8,4,64,576]{3,2,1,0:T(8,128)(2,1)}), bf16[8,4,64,576]{3,2,1,0:T(8,128)(2,1)}, u32[]{:S(2)}, u32[]{:S(2)}) %all-to-all-start.2) | async-done | bytes 2359328 | tf_op jit(solution)/shard_map/all_to_all | solution.py:36
  100.4 3.3 %pad_maximum_fusion = bf16[2,32,64,576]{3,2,1,0:T(8,128)(2,1)S(1)} fusion(bf16[1,32,64,576]{3,2,1,0:T(8,128)(2,1)} %bitcast.4), kind=kLoop, calls=%fused_computation.3 | loop fusion | flops 2359296 | bytes 7077888 | tf_op jit(solution)/shard_map/stack | solution.py:37
  103.7 12.3 %all_to_all.22 = bf16[2,32,64,576]{3,2,1,0:T(8,128)(2,1)S(1)} all-to-all(bf16[2,32,64,576]{3,2,1,0:T(8,128)(2,1)S(1)} %pad_maximum_fusion), channel_id=1, replica_groups=mesh['blk_0'=8,'blk_1'=4,'blk_2'=2,'head'=8] {'blk_2'}, dimensions={0} | all-to-all | bytes 9437184 | tf_op jit(solution)/shard_map/all_to_all | solution.py:36
  115.9 0.7 copy.27
  116.6 3.9 %fusion = (f32[512]{0:T(512)S(1)}, f32[512,4096]{1,0:T(8,128)S(1)}) fusion(s32[4096]{0:T(1024)S(1)} %fusion.37, s32[512]{0:T(512)S(1)} %le.16, bf16[4096,576]{1,0:T(8,128)(2,1)S(1)} %bitcast.33, bf16[64,8,576]{2,0,1:T(8,128)(2,1)S(1)} %pad_maximum_fusion.1), kind=kOutput, calls=%fused_computation.2 | convolution fusion | flops 2424307200 | bytes 13717504 | tf_op jit(solution)/shard_map/qd,kd->qk/dot_general | solution.py:122
  120.5 2.6 %fusion.1 = f32[512]{0:T(512)S(1)} fusion(f32[512,4096]{1,0:T(8,128)S(1)} %get-tuple-element.16, f32[512]{0:T(512)S(1)} %broadcast_maximum_fusion, s32[4096]{0:T(1024)S(1)} %fusion.37, s32[512]{0:T(512)S(1)} %le.16), kind=kLoop, calls=%fused_computation.4 | loop fusion | flops 12582400 | bytes 8411136 | tf_op jit(solution)/shard_map/reduce_sum | solution.py:129
  123.1 0.0 copy-start.1
  123.2 2.6 %fusion.17 = bf16[64,8,512]{2,1,0:T(8,128)(2,1)S(1)} fusion(bf16[4096,576]{1,0:T(8,128)(2,1)S(1)} %bitcast.34, f32[512,4096]{1,0:T(8,128)S(1)} %get-tuple-element.16, f32[512]{0:T(512)S(1)} %broadcast_maximum_fusion, s32[4096]{0:T(1024)S(1)} %fusion.37, s32[512]{0:T(512)S(1)} %le.16, f32[512]{0:T(512)S(1)} %fusion.1), kind=kOutput, calls=%fused_computation.20 | convolution fusion | flops 2160590848 | bytes 13129728 | tf_op jit(solution)/shard_map/dot_general | solution.py:130
  125.8 0.0 copy-done.1
  125.8 0.4 fusion.12
  126.2 0.7 copy.51
  (11 shorter events, 0.1 us)
Async XLA Ops:
  0.0 42.5 %copy-start = (bf16[8,128,512]{2,1,0:T(8,128)(2,1)S(1)}, bf16[8,128,512]{2,1,0:T(8,128)(2,1)}, u32[]{:S(2)}) copy-start(bf16[8,128,512]{2,1,0:T(8,128)(2,1)} %param.11) | copy-start | bytes 3145732
  0.0 41.6 %copy-start.4 = (s32[128]{0:T(128)S(1)}, s32[128]{0:T(128)}, u32[]{:S(2)}) copy-start(s32[128]{0:T(128)} %param.13) | copy-start | bytes 1540
  0.0 41.9 %copy-start.3 = (bf16[64,512]{1,0:T(8,128)(2,1)S(1)}, bf16[64,512]{1,0:T(8,128)(2,1)}, u32[]{:S(2)}) copy-start(bf16[64,512]{1,0:T(8,128)(2,1)} %param.8) | copy-start | bytes 196612
  0.0 42.5 %copy-start.2 = (bf16[64,1024]{1,0:T(8,128)(2,1)S(1)}, bf16[64,1024]{1,0:T(8,128)(2,1)}, u32[]{:S(2)}) copy-start(bf16[64,1024]{1,0:T(8,128)(2,1)} %param.7) | copy-start | bytes 393220
  34.7 65.6 %all-to-all-start.2 = ((bf16[8,4,64,576]{3,2,1,0:T(8,128)(2,1)}), bf16[8,4,64,576]{3,2,1,0:T(8,128)(2,1)}, u32[]{:S(2)}, u32[]{:S(2)}) async-start(bf16[8,4,64,576]{3,2,1,0:T(8,128)(2,1)} %stack.10), calls=%async_computation.2 | async-start | bytes 5242880 | tf_op jit(solution)/shard_map/all_to_all | solution.py:36
  123.1 2.6 %copy-start.1 = (bf16[8,512,128]{2,1,0:T(8,128)(2,1)S(1)}, bf16[8,512,128]{2,1,0:T(8,128)(2,1)}, u32[]{:S(2)}) copy-start(bf16[8,512,128]{2,1,0:T(8,128)(2,1)} %param.12) | copy-start | bytes 3145732
